TPU v7x, 256 devices: a whole 4x4x8 slice. The times are simulated.
256 devices in a mesh: owner: 64 (over x, z, core), dense: 4 (over y).
Axes of the slice: x: 4, y: 4, z: 8, core: 2. Of those that a mesh axis runs over, the one named last changes fastest.
Arguments:
- owners: int32 [65536, 13, 4], P(('owner', 'dense')), may hold values from 0 to 63, all different within a row; in each aligned block of 3328 rows (0 to 3327, 3328 to 6655, ..., all dimensions but the last counted through in order) at most 416 rows name the same one
- local_rows: int32 [65536, 13, 4], P(('owner', 'dense')), may hold values from 0 to 2047, as said below
- weights: float32 [65536, 13, 4], P(('owner', 'dense')), may hold values from 0.25 to 4
- labels: bfloat16 [65536], P(('owner', 'dense')), may hold values from 0 to 1
- table: float32 [131072, 128], P('owner'), may hold values from -6 to 6
- accum: float32 [131072], P('owner'), may hold values from 0.0001 to 0.01
- w_in: bfloat16 [1664, 4096], P(None, 'dense'), may hold values from -0.15625 to 0.15625
- b_in: bfloat16 [4096], P('dense'), may hold values from -3 to 3
- w_out: bfloat16 [4096], P('dense'), may hold values from -0.29882812 to 0.29882812
Outputs:
- new_table: float32 [131072, 128], P('owner')
- new_accum: float32 [131072], P('owner')
- weight_grad: float32 [65536, 13, 4], P(('owner', 'dense'))
Inputs may be any that keep to these rules, and one draw needn't show every extreme that they name: The 4 owners of one bag differ. Among the bags of one device (3328 of them, aligned blocks of rows), at most 416 name one owner. Among the ids of one device's samples (13312 of them, aligned blocks of rows), exactly 104 distinct values of local_rows occur.
All inputs are finite; a program needn't handle non-finite values.
Results may differ from a plain program's by a relative error of at most 0.0056.
Values may be sent and summed in bfloat16 or wider, within the bound.
No kernel may reach another device: no remote copies, remote signals or barrier semaphores. Data moves between devices by JAX's collectives and lax.ppermute only.
A program may use at most 128 MiB of HBM per device.

v0:
```python
import functools

import jax
import jax.numpy as jnp
from jax import lax
from jax.experimental import pallas as pl
from jax.experimental.pallas import tpu as pltpu
from jax.sharding import PartitionSpec as P

step_size = 0.5
UNIQ = 104
ROWS_DEV = 2048
LANES = 128
CHUNKS = ((0, 104),)
TAIL = 16
TAKE_BLOCK, POOL_STEP, GIVE_STEP, ADD_STEP, ALONG_STEP = 3328, 32, 16, 32, 8
HEAD_CUT, HEAD_MIB, STEP_MIB = 1024, 36, 32
MIB = 1024 * 1024
f32, bf16, i32 = jnp.float32, jnp.bfloat16, jnp.int32


def dot(a, b, dims=((1,), (0,))):
    return lax.dot_general(a, b, (dims, ((), ())), preferred_element_type=f32)


def params(mib, sem=None):
    return pltpu.CompilerParams(vmem_limit_bytes=mib * MIB, dimension_semantics=sem)


def cost(flops, moved=1 << 20):
    if moved == 0:
        return pl.CostEstimate(flops=flops, bytes_accessed=1 << 10, transcendentals=0)
    return pl.CostEstimate(flops=1 << 20, bytes_accessed=1 << 10, transcendentals=0)


def after(x, *before):
    return lax.optimization_barrier((x, *before))[0]


def marks_of(row, samples):
    lo = lax.broadcasted_iota(i32, (LANES, samples), 0) == (row & (LANES - 1))
    hi = lax.broadcasted_iota(i32, (ROWS_DEV // LANES, samples), 0) == (row >> 7)
    return jnp.where(lo, 1.0, 0.0).astype(bf16), jnp.where(hi, 1.0, 0.0)


def list_kernel(loc_ref, list_ref, rank_ref):
    fields, bag_len, samples = loc_ref.shape
    his = ROWS_DEV // LANES
    count = jnp.zeros((his, LANES), f32)
    for f in range(fields):
        for j in range(bag_len):
            lo, hi = marks_of(loc_ref[f, j : j + 1, :], samples)
            count = count + dot(hi.astype(bf16), lo, ((1,), (1,)))
    present = jnp.where(count > 0.5, 1.0, 0.0)
    tri = jnp.where(
        lax.broadcasted_iota(i32, (LANES, LANES), 0) <= lax.broadcasted_iota(i32, (LANES, LANES), 1), 1.0, 0.0
    ).astype(bf16)
    upto = dot(present.astype(bf16), tri)
    below = jnp.where(
        lax.broadcasted_iota(i32, (his, his), 0) > lax.broadcasted_iota(i32, (his, his), 1), 1.0, 0.0
    ).astype(bf16)
    totals = jnp.broadcast_to(upto[:, LANES - 1 :], (his, LANES))
    rank = upto - present + dot(below, totals.astype(bf16))
    rank_ref[...] = rank
    rank_cols = jnp.where(present > 0.5, rank, -1.0).T
    lane = lax.broadcasted_iota(i32, (LANES, LANES), 1).astype(f32)
    sub = lax.broadcasted_iota(i32, (LANES, LANES), 0).astype(f32)
    listed = jnp.zeros((LANES, LANES), f32)
    for h in range(his):
        listed = listed + jnp.where(rank_cols[:, h : h + 1] == lane, sub + float(h * LANES), 0.0)
    row = jnp.sum(listed, axis=0, keepdims=True).astype(i32)
    list_ref[...] = jnp.broadcast_to(row, list_ref.shape)


def list_call(loc, groups):
    return pl.pallas_call(
        list_kernel,
        out_shape=(
            jax.ShapeDtypeStruct((groups, LANES), i32),
            jax.ShapeDtypeStruct((ROWS_DEV // LANES, LANES), f32),
        ),
        compiler_params=params(16),
        cost_estimate=cost(1 << 31),
    )(loc)


def map_kernel(own_ref, loc_ref, w_ref, rank_ref, u_ref, c_ref):
    fields, bag_len, samples = own_ref.shape
    groups = u_ref.shape[0]
    rank_b = rank_ref[...].astype(bf16)
    own_iota = lax.broadcasted_iota(i32, (groups, samples), 0)

    def field(f, carry):
        loc, own, w = loc_ref[f], own_ref[f], w_ref[f]
        wsum = jnp.sum(w, axis=0, keepdims=True)
        u_map = jnp.full((groups, samples), -1.0, f32)
        c_map = jnp.zeros((groups, samples), f32)
        for j in range(bag_len):
            lo, hi = marks_of(loc[j : j + 1], samples)
            u = jnp.sum(dot(rank_b, lo) * hi, axis=0, keepdims=True)
            here = own_iota == own[j : j + 1]
            u_map = jnp.where(here, u, u_map)
            c_map = jnp.where(here, w[j : j + 1] / wsum, c_map)
        cols = pl.ds(pl.multiple_of(f * samples, samples), samples)
        u_ref[:, cols] = u_map
        c_ref[:, cols] = c_map
        return carry

    lax.fori_loop(0, fields, field, 0)


def map_call(own, loc, w, rank, groups):
    fields, _, samples = own.shape
    bags = fields * samples
    return pl.pallas_call(
        map_kernel,
        out_shape=(
            jax.ShapeDtypeStruct((groups, bags), f32),
            jax.ShapeDtypeStruct((groups, bags), f32),
        ),
        compiler_params=params(16),
        cost_estimate=cost(1 << 31),
    )(own, loc, w, rank)


def take_kernel(flat_ref, tb_ref, out_ref, tt_ref):
    rows, width = tb_ref.shape
    n = flat_ref.shape[1]

    @pl.when(pl.program_id(0) == 0)
    def _():
        tt_ref[...] = tb_ref[...].T.astype(bf16)

    part = 256
    for k in range(0, n, part):
        asked = flat_ref[:, k : k + part]
        marks = jnp.where(lax.broadcasted_iota(i32, (rows, part), 0) == asked, 1.0, 0.0).astype(bf16)
        out_ref[k : k + part, :] = dot(tt_ref[...], marks).T.astype(bf16)


def take_call(flat, table):
    n = flat.shape[1]
    rows, width = table.shape
    block = TAKE_BLOCK if n % TAKE_BLOCK == 0 else n
    return pl.pallas_call(
        take_kernel,
        grid=(n // block,),
        in_specs=[
            pl.BlockSpec((1, block), lambda i: (0, i)),
            pl.BlockSpec((rows, width), lambda i: (0, 0)),
        ],
        out_specs=pl.BlockSpec((block, width), lambda i: (i, 0)),
        out_shape=jax.ShapeDtypeStruct((n, width), bf16),
        scratch_shapes=[pltpu.VMEM((width, rows), bf16)],
        compiler_params=params(STEP_MIB, ("arbitrary",)),
        cost_estimate=cost(2 * n * rows * width * 2),
    )(flat, table)


def build(u_ref, c_ref, cols, first, count, lo, hi):
    n = hi - lo
    iota = lax.broadcasted_iota(i32, (n, cols.stop - cols.start), 0).astype(f32) + float(lo)
    return jnp.concatenate(
        [
            jnp.where(iota == u_ref[o : o + 1, cols], c_ref[o : o + 1, cols], 0.0)
            for o in range(first, first + count)
        ],
        axis=0,
    ).astype(bf16)


def steps_of(groups, most):
    return min(most, groups)


def pool_kernel(fields, lo, hi, first, last, u_ref, c_ref, r_ref, *refs):
    per_step, bags = u_ref.shape
    samples = bags // fields
    width = r_ref.shape[1]
    x_ref, acc_ref = refs[-2:] if last else (None, refs[-1])

    @pl.when(pl.program_id(0) == 0)
    def _():
        acc_ref[...] = jnp.zeros_like(acc_ref) if first else refs[0][...]

    rt = r_ref[...].astype(f32).T.astype(bf16)
    for f in range(fields):
        cols = slice(f * samples, (f + 1) * samples)
        acc_ref[:, cols] += dot(rt, build(u_ref, c_ref, cols, 0, per_step, lo, hi))

    if last:

        @pl.when(pl.program_id(0) == pl.num_programs(0) - 1)
        def _():
            for f in range(fields):
                x_ref[:, f * width : (f + 1) * width] = acc_ref[:, f * samples : (f + 1) * samples].T.astype(bf16)


def pool_call(u, c, r, fields, lo, hi, prev, last):
    groups, bags = u.shape
    width = r.shape[1]
    per_step = steps_of(groups, POOL_STEP)
    n = hi - lo
    acc = jax.ShapeDtypeStruct((width, bags), f32)
    x = jax.ShapeDtypeStruct((bags // fields, fields * width), bf16)
    acc_spec = pl.BlockSpec((width, bags), lambda i: (0, 0))
    return pl.pallas_call(
        functools.partial(pool_kernel, fields, lo, hi, prev is None, last),
        grid=(groups // per_step,),
        in_specs=[
            pl.BlockSpec((per_step, bags), lambda i: (i, 0)),
            pl.BlockSpec((per_step, bags), lambda i: (i, 0)),
            pl.BlockSpec((per_step * n, width), lambda i: (i, 0)),
        ]
        + ([] if prev is None else [acc_spec]),
        out_specs=pl.BlockSpec(x.shape, lambda i: (0, 0)) if last else acc_spec,
        out_shape=x if last else acc,
        scratch_shapes=[pltpu.VMEM((width, bags), f32)] if last else [],
        compiler_params=params(56, ("arbitrary",)),
        cost_estimate=cost(1<<34, 0),
    )(u, c, r, *([] if prev is None else [prev]))


def head_kernel(core_ref, x_ref, lab_ref, bw_ref, own_ref, near_ref, other_ref, far_ref, rest_ref, *refs):
    dt_ref, d_ref, slope_ref, acc_ref, held, sem = refs
    samples, ins = x_ref.shape
    width = d_ref.shape[1]
    hidden = own_ref.shape[1]
    half = far_ref.shape[0]
    core = core_ref[0]
    places = [
        (own_ref, held.at[0]),
        (near_ref, held.at[1]),
        (other_ref, held.at[2]),
        (far_ref, held.at[3, pl.ds(pl.multiple_of(core * half, half), half)]),
        (rest_ref, held.at[3, pl.ds(pl.multiple_of((1 - core) * half, half), half)]),
    ]
    copies = [pltpu.make_async_copy(a, b, sem.at[k]) for k, (a, b) in enumerate(places)]
    for copy in copies:
        copy.start()
    x = x_ref[...]
    logits = jnp.zeros((samples, 1), f32)
    cut = HEAD_CUT
    parts = [(b, slice(c, c + cut)) for b in range(4) for c in range(0, hidden, cut)]
    pre = None
    for k in range(len(parts) + 1):
        done = pre
        if k < len(parts):
            b, cols = parts[k]
            if cols.start == 0:
                copies[b].wait()
                if b == 3:
                    copies[4].wait()
            pre = dot(x, held[b, :, cols]) + bw_ref[b * TAIL : b * TAIL + 1, cols].astype(f32)
        if k > 0:
            b, cols = parts[k - 1]
            out = bw_ref[b * TAIL + 1 : b * TAIL + 2, cols].astype(f32)
            sig = jax.nn.sigmoid(done)
            logits = logits + jnp.sum(done * sig * out, axis=1, keepdims=True)
            slope_ref[b, :, cols] = (out * (sig * (1.0 + done * (1.0 - sig)))).astype(bf16)
    logits = jnp.broadcast_to(logits, (samples, LANES)).T[:1, :]
    grad = jax.nn.sigmoid(logits) - lab_ref[...]
    for b in range(4):
        part = dot(held[b], slope_ref[b], ((1,), (1,)))
        acc_ref[...] = part if b == 0 else acc_ref[...] + part
    for f in range(ins // width):
        block = acc_ref[f * width : (f + 1) * width, :] * grad
        dt_ref[f * width : (f + 1) * width, :] = block.astype(bf16)
        d_ref[f * samples : (f + 1) * samples, :] = block.T.astype(bf16)


def head_call(core, x, labels, bw, weights, width):
    samples, ins = x.shape
    hidden = weights[0].shape[1]
    vmem = pl.BlockSpec(memory_space=pltpu.VMEM)
    return pl.pallas_call(
        head_kernel,
        in_specs=[pl.BlockSpec(memory_space=pltpu.SMEM), vmem, vmem, vmem]
        + [pl.BlockSpec(memory_space=pl.ANY)] * len(weights),
        out_specs=(vmem, vmem),
        out_shape=(
            jax.ShapeDtypeStruct((ins, samples), bf16),
            jax.ShapeDtypeStruct((ins // width * samples, width), bf16),
        ),
        scratch_shapes=[
            pltpu.VMEM((4, samples, hidden), bf16),
            pltpu.VMEM((ins, samples), f32),
            pltpu.VMEM((4, ins, hidden), bf16),
            pltpu.SemaphoreType.DMA((len(weights),)),
        ],
        compiler_params=params(HEAD_MIB),
        cost_estimate=cost(4 * samples * ins * hidden * 4, 14 << 20),
    )(core, x, labels, bw, *weights)


def give_kernel(fields, lo, hi, u_ref, c_ref, d_ref, g_ref):
    per_step, bags = u_ref.shape
    samples = bags // fields
    total = None
    for f in range(fields):
        cols = slice(f * samples, (f + 1) * samples)
        got = dot(build(u_ref, c_ref, cols, 0, per_step, lo, hi), d_ref[cols, :])
        total = got if total is None else total + got
    g_ref[...] = total.astype(bf16)


def give_call(u, c, d, fields, lo, hi):
    groups, bags = u.shape
    width = d.shape[1]
    per_step = steps_of(groups, GIVE_STEP)
    n = hi - lo
    return pl.pallas_call(
        functools.partial(give_kernel, fields, lo, hi),
        grid=(groups // per_step,),
        in_specs=[
            pl.BlockSpec((per_step, bags), lambda i: (i, 0)),
            pl.BlockSpec((per_step, bags), lambda i: (i, 0)),
            pl.BlockSpec((bags, width), lambda i: (0, 0)),
        ],
        out_specs=pl.BlockSpec((per_step * n, width), lambda i: (i, 0)),
        out_shape=jax.ShapeDtypeStruct((groups * n, width), bf16),
        compiler_params=params(STEP_MIB, ("arbitrary",)),
        cost_estimate=cost(2 * groups * n * bags * width * 2),
    )(u, c, d)


def along_kernel(own_ref, w_ref, u_ref, dt_ref, *refs):
    r_refs, (out_ref, acc_ref) = refs[:-2], refs[-2:]
    fields, bag_len, samples = own_ref.shape
    per_step = u_ref.shape[0]
    width = r_refs[0].shape[1]
    step = pl.program_id(0)

    @pl.when(step == 0)
    def _():
        acc_ref[...] = jnp.zeros_like(acc_ref)

    def field(f, carry):
        cols = pl.ds(pl.multiple_of(f * samples, samples), samples)
        d = dt_ref[pl.ds(pl.multiple_of(f * width, width), width), :]
        prods = [dot(r_ref[...], d) for r_ref in r_refs]
        u = u_ref[:, cols]
        own = own_ref[f]
        got = acc_ref[f]
        for o in range(per_step):
            value = None
            for (lo, hi), prod in zip(CHUNKS, prods):
                n = hi - lo
                iota = lax.broadcasted_iota(i32, (n, samples), 0).astype(f32) + float(lo)
                hit = jnp.where(iota == u[o : o + 1], prod[o * n : (o + 1) * n, :], 0.0)
                part = jnp.sum(hit.reshape(n // 8, 8, samples), axis=0)
                value = part if value is None else value + part
            value = jnp.sum(value, axis=0, keepdims=True)
            got = jnp.where(own == step * per_step + o, value, got)
        acc_ref[f] = got
        return carry

    lax.fori_loop(0, fields, field, 0)

    @pl.when(step == pl.num_programs(0) - 1)
    def _():
        for f in range(fields):
            w = w_ref[f]
            wsum = jnp.sum(w, axis=0, keepdims=True)
            along = acc_ref[f]
            centre = jnp.sum(w * along, axis=0, keepdims=True) / wsum
            out_ref[f] = (along - centre) / wsum


def along_call(own, w, u, dt, rs):
    groups, bags = u.shape
    width = rs[0].shape[1]
    per_step = steps_of(groups, ALONG_STEP)
    whole3 = pl.BlockSpec(own.shape, lambda i: (0, 0, 0))
    return pl.pallas_call(
        along_kernel,
        grid=(groups // per_step,),
        in_specs=[
            whole3,
            whole3,
            pl.BlockSpec((per_step, bags), lambda i: (i, 0)),
            pl.BlockSpec(dt.shape, lambda i: (0, 0)),
        ]
        + [pl.BlockSpec((per_step * (hi - lo), width), lambda i: (i, 0)) for lo, hi in CHUNKS],
        out_specs=whole3,
        out_shape=jax.ShapeDtypeStruct(own.shape, f32),
        scratch_shapes=[pltpu.VMEM(own.shape, f32)],
        compiler_params=params(STEP_MIB, ("arbitrary",)),
        cost_estimate=cost(2 * groups * UNIQ * bags * width * 2),
    )(own, w, u, dt, *rs)


def add_kernel(first, last, lo, hi, list_ref, g_ref, *refs):
    out_ref, acc_ref = refs[-2:] if last else (None, refs[-1])
    width, rows = acc_ref.shape
    per_step = list_ref.shape[0]

    @pl.when(pl.program_id(0) == 0)
    def _():
        acc_ref[...] = jnp.zeros_like(acc_ref) if first else refs[0][...]

    asked = list_ref[...].T
    columns = jnp.concatenate([asked[lo:hi, o : o + 1] for o in range(per_step)], axis=0)
    gt = g_ref[...].astype(f32).T.astype(bf16)
    part = 256
    for k in range(0, rows, part):
        iota = lax.broadcasted_iota(i32, (columns.shape[0], part), 1) + k
        marks = jnp.where(iota == columns, 1.0, 0.0).astype(bf16)
        acc_ref[:, k : k + part] += dot(gt, marks)

    if last:

        @pl.when(pl.program_id(0) == pl.num_programs(0) - 1)
        def _():
            for k in range(0, rows, part):
                out_ref[k : k + part, :] = acc_ref[:, k : k + part].T.astype(bf16)


def add_call(lists, g, rows, lo, hi, prev, last):
    groups = lists.shape[0]
    width = g.shape[1]
    per_step = steps_of(groups, ADD_STEP)
    acc = pl.BlockSpec((width, rows), lambda i: (0, 0))
    return pl.pallas_call(
        functools.partial(add_kernel, prev is None, last, lo, hi),
        grid=(groups // per_step,),
        in_specs=[
            pl.BlockSpec((per_step, LANES), lambda i: (i, 0)),
            pl.BlockSpec((per_step * (hi - lo), width), lambda i: (i, 0)),
        ]
        + ([] if prev is None else [acc]),
        out_specs=pl.BlockSpec((rows, width), lambda i: (0, 0)) if last else acc,
        out_shape=jax.ShapeDtypeStruct((rows, width), bf16) if last else jax.ShapeDtypeStruct((width, rows), f32),
        scratch_shapes=[pltpu.VMEM((width, rows), f32)] if last else [],
        compiler_params=params(STEP_MIB, ("arbitrary",)),
        cost_estimate=cost(2 * g.shape[0] * rows * width * 2),
    )(lists, g, *([] if prev is None else [prev]))


def send(x, groups):
    width = x.shape[1]
    return lax.all_to_all(
        x.reshape(groups, -1, width), "owner", split_axis=0, concat_axis=0, tiled=True
    ).reshape(-1, width)


def turn(x, shift):
    dense = lax.axis_size("dense")
    return lax.ppermute(x, "dense", [(i, (i + shift) % dense) for i in range(dense)])


def hop(x):
    groups, dense = lax.axis_size("owner"), lax.axis_size("dense")
    pairs = [(o * dense + q, o * dense + (q + 1 - 2 * (o % 2)) % dense) for o in range(groups) for q in range(dense)]
    return lax.ppermute(x, ("owner", "dense"), pairs)


def swap(x):
    return lax.ppermute(x, "owner", [(i, i ^ 1) for i in range(lax.axis_size("owner"))])


def local(owners, local_rows, weights, labels, table, accum, w_in, b_in, w_out):
    fields = owners.shape[1]
    rows, width = table.shape
    groups = lax.axis_size("owner")
    dense = lax.axis_size("dense")
    own, loc, w = (a.transpose(1, 2, 0) for a in (owners, local_rows, weights))

    near = hop(w_in)
    listed, rank = list_call(loc, groups)
    lists = lax.all_to_all(listed, "owner", split_axis=0, concat_axis=0, tiled=True)
    flat = [lists[:, lo:hi].reshape(1, groups * (hi - lo)) for lo, hi in CHUNKS]
    found = [take_call(a, table) for a in flat]
    rs = [send(x, groups) for x in found]
    u, c = map_call(own, loc, w, after(rank, *found), groups)

    core = (lax.axis_index("owner") % 2).astype(i32)
    half = w_in.shape[0] // 2
    near = after(near, u)
    far = hop(lax.dynamic_slice_in_dim(near, core * half, half, axis=0))
    bw = jnp.concatenate([b_in[None], w_out[None], jnp.zeros((TAIL - 2, w_in.shape[1]), bf16)], axis=0)
    bw = after(bw, u)
    bw_near = hop(bw)
    bw = jnp.concatenate([bw, bw_near, swap(bw_near), hop(bw_near)], axis=0)
    other = swap(near)
    rest = swap(far)
    head_weights = [w_in, near, other, far, rest]

    x = None
    for k, (lo, hi) in enumerate(CHUNKS):
        x = pool_call(u, c, after(rs[k], far), fields, lo, hi, x, k == len(CHUNKS) - 1)
    dt, d = head_call(core[None], x, labels.astype(f32)[None], bw, head_weights, width)
    gs = [give_call(u, c, d, fields, lo, hi) for lo, hi in CHUNKS]
    gots = [send(g, groups) for g in gs]
    weight_grad = along_call(own, w, u, after(dt, *gs), rs)
    part = None
    for k, (lo, hi) in enumerate(CHUNKS):
        got = after(gots[k], weight_grad) if k == 0 else gots[k]
        part = add_call(lists, got, rows, lo, hi, part, k == len(CHUNKS) - 1)

    cut = rows // dense
    me = lax.axis_index("dense")
    piece = lambda k: lax.dynamic_slice_in_dim(part, lax.rem(me + k, dense) * cut, cut, axis=0)
    total = piece(0).astype(f32)
    for k in range(1, dense):
        total = total + turn(piece(k), k).astype(f32)
    total = total.astype(bf16)
    row_grad = jnp.zeros((rows, width), bf16)
    for k in range(dense):
        got = total if k == 0 else turn(total, k)
        row_grad = lax.dynamic_update_slice_in_dim(row_grad, got, lax.rem(me + dense - k, dense) * cut, axis=0)
    row_grad = row_grad.astype(f32)
    new_accum = accum + jnp.mean(row_grad * row_grad, axis=-1)
    new_table = table - step_size * row_grad / jnp.sqrt(new_accum)[:, None]
    return (new_table, new_accum, weight_grad.transpose(2, 0, 1))


def solution(mesh):
    placed = (
        P(("owner", "dense"), None, None),
        P(("owner", "dense"), None, None),
        P(("owner", "dense"), None, None),
        P(("owner", "dense")),
        P("owner", None),
        P("owner"),
        P(None, "dense"),
        P("dense"),
        P("dense"),
    )
    return jax.shard_map(
        local,
        mesh=mesh,
        in_specs=placed,
        out_specs=(P("owner", None), P("owner"), P(("owner", "dense"), None, None)),
        check_vma=False,
    )
```

profile of v0, /device:TPU:1, one launch (start us, length us, event | category | flops | bytes accessed | tf_op | source)
XLA Modules:
  0.0 194.1 jit_solution(2481250768694668358)
XLA Ops:
  0.6 3.6 %collective-permute-start = (bf16[1664,1024]{1,0:T(8,128)(2,1)}, bf16[1664,1024]{1,0:T(8,128)(2,1)S(1)}, u32[]{:S(2)}, u32[]{:S(2)}) collective-permute-start(bf16[1664,1024]{1,0:T(8,128)(2,1)} %own_ref.1), channel_id=1, source_target_pairs={{0,1},{1,2},{2,3},{3,0},{4,7},{5,4},{6,5},{7,6},{8,9},{9,10},{10,1... | collective-permute-start | bytes 10223624 | tf_op jit(solution)/shard_map/ppermute | solution.py:455
  5.1 1.9 shard_map.112
  6.9 20.7 %all_to_all.21 = s32[64,1,128]{2,1,0:T(1,128)S(1)} all-to-all(s32[64,1,128]{2,1,0:T(1,128)S(1)} %bitcast.25), channel_id=1, replica_groups=mesh['owner'=64,'dense'=4] {'owner'}, dimensions={0} | all-to-all | bytes 65536 | tf_op jit(solution)/shard_map/all_to_all | solution.py:471
  27.7 1.2 copy-done.1
  29.0 4.8 %shard_map.113 = bf16[6656,128]{1,0:T(8,128)(2,1)S(1)} custom-call(s32[1,6656]{1,0:T(1,128)S(1)} %reshape.24.flat_ref, f32[2048,128]{1,0:T(8,128)S(1)} %copy-done.1), custom_call_target="tpu_custom_call" | custom-call | flops 1048576 | bytes 1024 | tf_op jit(solution)/shard_map/pallas_call | solution.py:145
  33.8 1.2 copy-done
  35.0 5.7 %all-to-all-start.1 = ((bf16[64,104,128]{2,1,0:T(8,128)(2,1)}), bf16[64,104,128]{2,1,0:T(8,128)(2,1)}, u32[]{:S(2)}, u32[]{:S(2)}) async-start(bf16[64,104,128]{2,1,0:T(8,128)(2,1)} %bitcast.15), calls=%async_computation.1 | async-start | bytes 3407872 | tf_op jit(solution)/shard_map/all_to_all | solution.py:442
  41.5 2.3 %shard_map.114 = (f32[64,3328]{1,0:T(8,128)S(1)}, f32[64,3328]{1,0:T(8,128)S(1)}) custom-call(s32[13,4,256]{2,1,0:T(4,128)S(1)} %bitcast.19, s32[13,4,256]{2,1,0:T(4,128)S(1)} %bitcast.24, f32[13,4,256]{2,1,0:T(4,128)S(1)} %bitcast.21, f32[16,128]{1,0:T(8,128)S(1)} %get-tuple-element.17.rank_ref), custom_call_target="tpu_custom_call" | custom-call | flops 1048576 | bytes 1024 | tf_op jit(solution)/shard_map/pallas_call | solution.py:115
  43.8 0.9 copy-done.4
  44.7 0.9 copy-done.10
  45.8 0.9 collective-permute-start.1
  47.6 2.0 %collective-permute-start.2 = (bf16[16,1024]{1,0:T(8,128)(2,1)S(1)}, bf16[16,1024]{1,0:T(8,128)(2,1)S(1)}, u32[]{:S(2)}, u32[]{:S(2)}) collective-permute-start(bf16[16,1024]{1,0:T(8,128)(2,1)S(1)} %maximum_maximum_fusion), channel_id=1, source_target_pairs={{0,1},{1,2},{2,3},{3,0},{4,7},{5,4},{6,5},{7,6},{8,9},{9,10},{10,1... | collective-permute-start | bytes 98312 | tf_op jit(solution)/shard_map/ppermute | solution.py:455
  49.6 17.6 %collective-permute-done.2 = bf16[16,1024]{1,0:T(8,128)(2,1)S(1)} collective-permute-done((bf16[16,1024]{1,0:T(8,128)(2,1)S(1)}, bf16[16,1024]{1,0:T(8,128)(2,1)S(1)}, u32[]{:S(2)}, u32[]{:S(2)}) %collective-permute-start.2) | collective-permute-done | bytes 32800 | tf_op jit(solution)/shard_map/ppermute | solution.py:455
  67.3 2.6 %collective-permute-start.3 = (bf16[16,1024]{1,0:T(8,128)(2,1)S(1)}, bf16[16,1024]{1,0:T(8,128)(2,1)S(1)}, u32[]{:S(2)}, u32[]{:S(2)}) collective-permute-start(bf16[16,1024]{1,0:T(8,128)(2,1)S(1)} %collective-permute-done.2), channel_id=1, source_target_pairs={{0,4},{4,0},{8,12},{12,8},{16,20},{20,16},{24,28},{28,24},{32,36},... | collective-permute-start | bytes 98312 | tf_op jit(solution)/shard_map/ppermute | solution.py:459
  70.7 2.3 %collective-permute-done.4 = bf16[16,1024]{1,0:T(8,128)(2,1)S(1)} collective-permute-done((bf16[16,1024]{1,0:T(8,128)(2,1)S(1)}, bf16[16,1024]{1,0:T(8,128)(2,1)S(1)}, u32[]{:S(2)}, u32[]{:S(2)}) %collective-permute-start.4) | collective-permute-done | bytes 32800 | tf_op jit(solution)/shard_map/ppermute | solution.py:455
  73.0 10.2 %all-to-all-done.1 = bf16[64,104,128]{2,1,0:T(8,128)(2,1)} async-done(((bf16[64,104,128]{2,1,0:T(8,128)(2,1)}), bf16[64,104,128]{2,1,0:T(8,128)(2,1)}, u32[]{:S(2)}, u32[]{:S(2)}) %all-to-all-start.1) | async-done | bytes 1703968 | tf_op jit(solution)/shard_map/all_to_all | solution.py:442
  83.2 9.2 %shard_map.115.x_ref = bf16[256,1664]{1,0:T(8,128)(2,1)} custom-call(f32[64,3328]{1,0:T(8,128)} %copy-done.4, f32[64,3328]{1,0:T(8,128)} %copy-done.10, bf16[6656,128]{1,0:T(8,128)(2,1)} %bitcast.8.r_ref.refs_0_), custom_call_target="tpu_custom_call" | custom-call | flops 17179869184 | bytes 1024 | tf_op jit(solution)/shard_map/pallas_call | solution.py:207
  92.4 1.1 copy-done.7
  93.6 9.7 %shard_map.116 = (bf16[1664,256]{1,0:T(8,128)(2,1)S(1)}, bf16[3328,128]{1,0:T(8,128)(2,1)S(1)}) custom-call(s32[1]{0:T(128)} %bitcast.6.core_ref, bf16[256,1664]{1,0:T(8,128)(2,1)S(1)} %copy-done.7, f32[1,256]{1,0:T(1,128)S(1)} %bitcast.26, bf16[64,1024]{1,0:T(8,128)(2,1)S(1)} %pad_maximum_fusion.bw_ref, bf16[1664,1024]{1,0:T(8,128)(2,1)S(1)} %copy-done.3, ...), custom_call_target="tpu_custom_call" | custom-call | flops 1048576 | bytes 1024 | tf_op jit(solution)/shard_map/pallas_call | solution.py:276
  103.3 13.2 %shard_map.117 = bf16[6656,128]{1,0:T(8,128)(2,1)} custom-call(f32[64,3328]{1,0:T(8,128)S(1)} %copy-done.5, f32[64,3328]{1,0:T(8,128)S(1)} %copy-done.11, bf16[3328,128]{1,0:T(8,128)(2,1)S(1)} %get-tuple-element.23.d_ref), custom_call_target="tpu_custom_call" | custom-call | flops 1048576 | bytes 1024 | tf_op jit(solution)/shard_map/pallas_call | solution.py:312
  116.6 6.3 %all-to-all-start.2 = ((bf16[64,104,128]{2,1,0:T(8,128)(2,1)}), bf16[64,104,128]{2,1,0:T(8,128)(2,1)S(1)}, u32[]{:S(2)}, u32[]{:S(2)}) async-start(bf16[64,104,128]{2,1,0:T(8,128)(2,1)} %bitcast.10), calls=%async_computation.2 | async-start | bytes 3407872 | tf_op jit(solution)/shard_map/all_to_all | solution.py:442
  123.0 29.9 %shard_map.118 = f32[13,4,256]{2,1,0:T(4,128)} custom-call(s32[13,4,256]{2,1,0:T(4,128)S(1)} %bitcast.20, f32[13,4,256]{2,1,0:T(4,128)S(1)} %bitcast.22, f32[64,3328]{1,0:T(8,128)S(1)} %copy-done.6, bf16[1664,256]{1,0:T(8,128)(2,1)S(1)} %copy-done.9, bf16[6656,128]{1,0:T(8,128)(2,1)} %bitcast.8.r_ref.refs_0_), custom_call_target="tpu_custom_call" | custom-call | flops 1048576 | bytes 1024 | tf_op jit(solution)/shard_map/pallas_call | solution.py:375
  152.8 12.7 %all-to-all-done.2 = bf16[64,104,128]{2,1,0:T(8,128)(2,1)S(1)} async-done(((bf16[64,104,128]{2,1,0:T(8,128)(2,1)}), bf16[64,104,128]{2,1,0:T(8,128)(2,1)S(1)}, u32[]{:S(2)}, u32[]{:S(2)}) %all-to-all-start.2) | async-done | bytes 1703968 | tf_op jit(solution)/shard_map/all_to_all | solution.py:442
  165.5 6.4 %shard_map.119 = bf16[2048,128]{1,0:T(8,128)(2,1)S(1)} custom-call(s32[64,128]{1,0:T(8,128)S(1)} %bitcast.18, bf16[6656,128]{1,0:T(8,128)(2,1)S(1)} %bitcast.16), custom_call_target="tpu_custom_call" | custom-call | flops 1048576 | bytes 1024 | tf_op jit(solution)/shard_map/pallas_call | solution.py:424
  172.7 1.4 collective-permute-start.8
  174.1 2.0 %collective-permute-start.9 = (bf16[512,128]{1,0:T(8,128)(2,1)S(1)}, bf16[512,128]{1,0:T(8,128)(2,1)S(1)}, u32[]{:S(2)}, u32[]{:S(2)}) collective-permute-start(bf16[512,128]{1,0:T(8,128)(2,1)S(1)} %get-tuple-element.32), channel_id=1, source_target_pairs={{0,3},{1,0},{2,1},{3,2},{4,7},{5,4},{6,5},{7,6},{8,11},{9,8},{10,9... | collective-permute-start | bytes 393224 | tf_op jit(solution)/shard_map/ppermute | solution.py:449
  176.1 5.0 %collective-permute-done.7 = bf16[512,128]{1,0:T(8,128)(2,1)S(1)} collective-permute-done((bf16[512,128]{1,0:T(8,128)(2,1)S(1)}, bf16[512,128]{1,0:T(8,128)(2,1)S(1)}, u32[]{:S(2)}, u32[]{:S(2)}) %collective-permute-start.7) | collective-permute-done | bytes 131104 | tf_op jit(solution)/shard_map/ppermute | solution.py:449
  181.5 2.2 %collective-permute-start.10 = (bf16[512,128]{1,0:T(8,128)(2,1)S(1)}, bf16[512,128]{1,0:T(8,128)(2,1)S(1)}, u32[]{:S(2)}, u32[]{:S(2)}) collective-permute-start(bf16[512,128]{1,0:T(8,128)(2,1)S(1)} %get-tuple-element.30), channel_id=1, source_target_pairs={{0,1},{1,2},{2,3},{3,0},{4,5},{5,6},{6,7},{7,4},{8,9},{9,10},{10,1... | collective-permute-start | bytes 393224 | tf_op jit(solution)/shard_map/ppermute | solution.py:449
  183.7 2.2 %collective-permute-start.11 = (bf16[512,128]{1,0:T(8,128)(2,1)S(1)}, bf16[512,128]{1,0:T(8,128)(2,1)S(1)}, u32[]{:S(2)}, u32[]{:S(2)}) collective-permute-start(bf16[512,128]{1,0:T(8,128)(2,1)S(1)} %get-tuple-element.30), channel_id=1, source_target_pairs={{0,2},{1,3},{2,0},{3,1},{4,6},{5,7},{6,4},{7,5},{8,10},{9,11},{10,... | collective-permute-start | bytes 393224 | tf_op jit(solution)/shard_map/ppermute | solution.py:449
  186.2 1.3 collective-permute-done.10
  187.5 4.3 %collective-permute-done.11 = bf16[512,128]{1,0:T(8,128)(2,1)S(1)} collective-permute-done((bf16[512,128]{1,0:T(8,128)(2,1)S(1)}, bf16[512,128]{1,0:T(8,128)(2,1)S(1)}, u32[]{:S(2)}, u32[]{:S(2)}) %collective-permute-start.11) | collective-permute-done | bytes 131104 | tf_op jit(solution)/shard_map/ppermute | solution.py:449
  192.8 1.3 fusion.1
  (73 shorter events, 6.4 us)
Async XLA Ops:
  0.6 45.0 %collective-permute-start = (bf16[1664,1024]{1,0:T(8,128)(2,1)}, bf16[1664,1024]{1,0:T(8,128)(2,1)S(1)}, u32[]{:S(2)}, u32[]{:S(2)}) collective-permute-start(bf16[1664,1024]{1,0:T(8,128)(2,1)} %own_ref.1), channel_id=1, source_target_pairs={{0,1},{1,2},{2,3},{3,0},{4,7},{5,4},{6,5},{7,6},{8,9},{9,10},{10,1... | collective-permute-start | bytes 10223624 | tf_op jit(solution)/shard_map/ppermute | solution.py:455
  27.6 7.3 %copy-start.12 = (s32[64,1,128]{2,1,0:T(1,128)}, s32[64,1,128]{2,1,0:T(1,128)S(1)}, u32[]{:S(2)}) copy-start(s32[64,1,128]{2,1,0:T(1,128)S(1)} %all_to_all.21) | copy-start | bytes 98308
  34.9 5.7 %copy-start.14 = (s32[256,13,4]{0,2,1:T(4,128)S(1)}, s32[256,13,4]{0,2,1:T(4,128)}, u32[]{:S(2)}) copy-start(s32[256,13,4]{0,2,1:T(4,128)} %param.9) | copy-start | bytes 159748
  34.9 5.7 %copy-start.16 = (f32[256,13,4]{0,2,1:T(4,128)S(1)}, f32[256,13,4]{0,2,1:T(4,128)}, u32[]{:S(2)}) copy-start(f32[256,13,4]{0,2,1:T(4,128)} %param.11) | copy-start | bytes 159748
  35.0 48.3 %all-to-all-start.1 = ((bf16[64,104,128]{2,1,0:T(8,128)(2,1)}), bf16[64,104,128]{2,1,0:T(8,128)(2,1)}, u32[]{:S(2)}, u32[]{:S(2)}) async-start(bf16[64,104,128]{2,1,0:T(8,128)(2,1)} %bitcast.15), calls=%async_computation.1 | async-start | bytes 3407872 | tf_op jit(solution)/shard_map/all_to_all | solution.py:442
  45.6 1.9 copy-start.21
  45.6 1.9 copy-start.22
  45.6 24.3 %copy-start.23 = (bf16[256]{0:T(256)(128)(2,1)S(1)}, bf16[256]{0:T(256)(128)(2,1)}, u32[]{:S(2)}) copy-start(bf16[256]{0:T(256)(128)(2,1)} %param.12) | copy-start | bytes 1540
  45.8 24.1 %collective-permute-start.1 = (bf16[832,1024]{1,0:T(8,128)(2,1)S(1)}, bf16[832,1024]{1,0:T(8,128)(2,1)}, u32[]{:S(2)}, u32[]{:S(2)}) collective-permute-start(bf16[832,1024]{1,0:T(8,128)(2,1)S(1)} %constant_dynamic-slice_fusion.3), channel_id=1, source_target_pairs={{0,1},{1,2},{2,3},{3,0},{4,7},{5,4},{6,5},{7,6},{8,9},{9,10},{10,1... | collective-permute-start | bytes 5111816 | tf_op jit(solution)/shard_map/ppermute | solution.py:455
  46.6 45.8 %collective-permute-start.5 = (bf16[1664,1024]{1,0:T(8,128)(2,1)S(1)}, bf16[1664,1024]{1,0:T(8,128)(2,1)}, u32[]{:S(2)}, u32[]{:S(2)}) collective-permute-start(bf16[1664,1024]{1,0:T(8,128)(2,1)S(1)} %collective-permute-done.near_ref), channel_id=1, source_target_pairs={{0,4},{4,0},{8,12},{12,8},{16,20},{20,16},{24,28},{28,24},{32,36},... | collective-permute-start | bytes 10223624 | tf_op jit(solution)/shard_map/ppermute | solution.py:459
  47.6 19.6 %collective-permute-start.2 = (bf16[16,1024]{1,0:T(8,128)(2,1)S(1)}, bf16[16,1024]{1,0:T(8,128)(2,1)S(1)}, u32[]{:S(2)}, u32[]{:S(2)}) collective-permute-start(bf16[16,1024]{1,0:T(8,128)(2,1)S(1)} %maximum_maximum_fusion), channel_id=1, source_target_pairs={{0,1},{1,2},{2,3},{3,0},{4,7},{5,4},{6,5},{7,6},{8,9},{9,10},{10,1... | collective-permute-start | bytes 98312 | tf_op jit(solution)/shard_map/ppermute | solution.py:455
  67.3 3.5 %collective-permute-start.3 = (bf16[16,1024]{1,0:T(8,128)(2,1)S(1)}, bf16[16,1024]{1,0:T(8,128)(2,1)S(1)}, u32[]{:S(2)}, u32[]{:S(2)}) collective-permute-start(bf16[16,1024]{1,0:T(8,128)(2,1)S(1)} %collective-permute-done.2), channel_id=1, source_target_pairs={{0,4},{4,0},{8,12},{12,8},{16,20},{20,16},{24,28},{28,24},{32,36},... | collective-permute-start | bytes 98312 | tf_op jit(solution)/shard_map/ppermute | solution.py:459
  69.8 3.2 %collective-permute-start.4 = (bf16[16,1024]{1,0:T(8,128)(2,1)S(1)}, bf16[16,1024]{1,0:T(8,128)(2,1)S(1)}, u32[]{:S(2)}, u32[]{:S(2)}) collective-permute-start(bf16[16,1024]{1,0:T(8,128)(2,1)S(1)} %collective-permute-done.2), channel_id=1, source_target_pairs={{0,1},{1,2},{2,3},{3,0},{4,7},{5,4},{6,5},{7,6},{8,9},{9,10},{10,1... | collective-permute-start | bytes 98312 | tf_op jit(solution)/shard_map/ppermute | solution.py:455
  69.9 22.5 %collective-permute-start.6 = (bf16[832,1024]{1,0:T(8,128)(2,1)}, bf16[832,1024]{1,0:T(8,128)(2,1)}, u32[]{:S(2)}, u32[]{:S(2)}) collective-permute-start(bf16[832,1024]{1,0:T(8,128)(2,1)} %collective-permute-done.1.far_ref), channel_id=1, source_target_pairs={{0,4},{4,0},{8,12},{12,8},{16,20},{20,16},{24,28},{28,24},{32,36},... | collective-permute-start | bytes 5111816 | tf_op jit(solution)/shard_map/ppermute | solution.py:459
  83.2 9.2 %copy-start.3 = (bf16[1664,1024]{1,0:T(8,128)(2,1)S(1)}, bf16[1664,1024]{1,0:T(8,128)(2,1)}, u32[]{:S(2)}) copy-start(bf16[1664,1024]{1,0:T(8,128)(2,1)} %own_ref.1) | copy-start | bytes 10223620
  93.6 9.7 %copy-start.5 = (f32[64,3328]{1,0:T(8,128)S(1)}, f32[64,3328]{1,0:T(8,128)}, u32[]{:S(2)}) copy-start(f32[64,3328]{1,0:T(8,128)} %copy-done.4) | copy-start | bytes 2555908
  93.6 9.7 %copy-start.11 = (f32[64,3328]{1,0:T(8,128)S(1)}, f32[64,3328]{1,0:T(8,128)}, u32[]{:S(2)}) copy-start(f32[64,3328]{1,0:T(8,128)} %copy-done.10) | copy-start | bytes 2555908
  103.3 13.3 %copy-start.8 = (bf16[1664,256]{1,0:T(8,128)(2,1)}, bf16[1664,256]{1,0:T(8,128)(2,1)S(1)}, u32[]{:S(2)}) copy-start(bf16[1664,256]{1,0:T(8,128)(2,1)S(1)} %get-tuple-element.25.dt_ref) | copy-start | bytes 2555908
  116.6 6.4 %copy-start.6 = (f32[64,3328]{1,0:T(8,128)S(1)}, f32[64,3328]{1,0:T(8,128)}, u32[]{:S(2)}) copy-start(f32[64,3328]{1,0:T(8,128)} %copy-done.4) | copy-start | bytes 2555908
  116.6 6.4 %copy-start.9 = (bf16[1664,256]{1,0:T(8,128)(2,1)S(1)}, bf16[1664,256]{1,0:T(8,128)(2,1)}, u32[]{:S(2)}) copy-start(bf16[1664,256]{1,0:T(8,128)(2,1)} %copy-done.8) | copy-start | bytes 2555908
  116.6 6.4 %copy-start.15 = (s32[256,13,4]{0,2,1:T(4,128)S(1)}, s32[256,13,4]{0,2,1:T(4,128)}, u32[]{:S(2)}) copy-start(s32[256,13,4]{0,2,1:T(4,128)} %param.9) | copy-start | bytes 159748
  116.6 6.4 %copy-start.17 = (f32[256,13,4]{0,2,1:T(4,128)S(1)}, f32[256,13,4]{0,2,1:T(4,128)}, u32[]{:S(2)}) copy-start(f32[256,13,4]{0,2,1:T(4,128)} %param.11) | copy-start | bytes 159748
  116.6 48.9 %all-to-all-start.2 = ((bf16[64,104,128]{2,1,0:T(8,128)(2,1)}), bf16[64,104,128]{2,1,0:T(8,128)(2,1)S(1)}, u32[]{:S(2)}, u32[]{:S(2)}) async-start(bf16[64,104,128]{2,1,0:T(8,128)(2,1)} %bitcast.10), calls=%async_computation.2 | async-start | bytes 3407872 | tf_op jit(solution)/shard_map/all_to_all | solution.py:442
  123.0 42.5 %copy-start.13 = (s32[64,1,128]{2,1,0:T(1,128)S(1)}, s32[64,1,128]{2,1,0:T(1,128)}, u32[]{:S(2)}) copy-start(s32[64,1,128]{2,1,0:T(1,128)} %copy-done.12) | copy-start | bytes 98308
  171.9 20.3 %copy-start.20 = (f32[2048]{0:T(1024)S(1)}, f32[2048]{0:T(1024)}, u32[]{:S(2)}) copy-start(f32[2048]{0:T(1024)} %param.14) | copy-start | bytes 24580
  171.9 20.9 %copy-start.2 = (f32[2048,128]{1,0:T(8,128)S(1)}, f32[2048,128]{1,0:T(8,128)}, u32[]{:S(2)}) copy-start(f32[2048,128]{1,0:T(8,128)} %tb_ref.1) | copy-start | bytes 3145732
  171.9 9.2 %collective-permute-start.7 = (bf16[512,128]{1,0:T(8,128)(2,1)S(1)}, bf16[512,128]{1,0:T(8,128)(2,1)S(1)}, u32[]{:S(2)}, u32[]{:S(2)}) collective-permute-start(bf16[512,128]{1,0:T(8,128)(2,1)S(1)} %get-tuple-element.31), channel_id=1, source_target_pairs={{0,1},{1,2},{2,3},{3,0},{4,5},{5,6},{6,7},{7,4},{8,9},{9,10},{10,1... | collective-permute-start | bytes 393224 | tf_op jit(solution)/shard_map/ppermute | solution.py:449
  172.7 8.4 %collective-permute-start.8 = (bf16[512,128]{1,0:T(8,128)(2,1)S(1)}, bf16[512,128]{1,0:T(8,128)(2,1)S(1)}, u32[]{:S(2)}, u32[]{:S(2)}) collective-permute-start(bf16[512,128]{1,0:T(8,128)(2,1)S(1)} %get-tuple-element.33), channel_id=1, source_target_pairs={{0,2},{1,3},{2,0},{3,1},{4,6},{5,7},{6,4},{7,5},{8,10},{9,11},{10,... | collective-permute-start | bytes 393224 | tf_op jit(solution)/shard_map/ppermute | solution.py:449
  174.1 7.2 %collective-permute-start.9 = (bf16[512,128]{1,0:T(8,128)(2,1)S(1)}, bf16[512,128]{1,0:T(8,128)(2,1)S(1)}, u32[]{:S(2)}, u32[]{:S(2)}) collective-permute-start(bf16[512,128]{1,0:T(8,128)(2,1)S(1)} %get-tuple-element.32), channel_id=1, source_target_pairs={{0,3},{1,0},{2,1},{3,2},{4,7},{5,4},{6,5},{7,6},{8,11},{9,8},{10,9... | collective-permute-start | bytes 393224 | tf_op jit(solution)/shard_map/ppermute | solution.py:449
  181.5 5.9 %collective-permute-start.10 = (bf16[512,128]{1,0:T(8,128)(2,1)S(1)}, bf16[512,128]{1,0:T(8,128)(2,1)S(1)}, u32[]{:S(2)}, u32[]{:S(2)}) collective-permute-start(bf16[512,128]{1,0:T(8,128)(2,1)S(1)} %get-tuple-element.30), channel_id=1, source_target_pairs={{0,1},{1,2},{2,3},{3,0},{4,5},{5,6},{6,7},{7,4},{8,9},{9,10},{10,1... | collective-permute-start | bytes 393224 | tf_op jit(solution)/shard_map/ppermute | solution.py:449
  183.7 8.1 %collective-permute-start.11 = (bf16[512,128]{1,0:T(8,128)(2,1)S(1)}, bf16[512,128]{1,0:T(8,128)(2,1)S(1)}, u32[]{:S(2)}, u32[]{:S(2)}) collective-permute-start(bf16[512,128]{1,0:T(8,128)(2,1)S(1)} %get-tuple-element.30), channel_id=1, source_target_pairs={{0,2},{1,3},{2,0},{3,1},{4,6},{5,7},{6,4},{7,5},{8,10},{9,11},{10,... | collective-permute-start | bytes 393224 | tf_op jit(solution)/shard_map/ppermute | solution.py:449
  185.9 5.9 %collective-permute-start.12 = (bf16[512,128]{1,0:T(8,128)(2,1)S(1)}, bf16[512,128]{1,0:T(8,128)(2,1)S(1)}, u32[]{:S(2)}, u32[]{:S(2)}) collective-permute-start(bf16[512,128]{1,0:T(8,128)(2,1)S(1)} %get-tuple-element.30), channel_id=1, source_target_pairs={{0,3},{1,0},{2,1},{3,2},{4,7},{5,4},{6,5},{7,6},{8,11},{9,8},{10,9... | collective-permute-start | bytes 393224 | tf_op jit(solution)/shard_map/ppermute | solution.py:449
  (7 other events, 7.0 us)
where the time goes:
time: 195 us; the launch traced here: 194 us
  Pallas kernels  77.2 us (40%)
  waiting for transfers between devices  54.1 us (28%)
  starting transfers between devices  31.1 us (16%)
  blocking collectives  20.7 us (11%)
  local copies, waits for them, and re-layouts  7.57 us (4%)
  other arithmetic  2.46 us (1%)
    pallas_call x1, Pallas kernels, along_call(): pl.pallas_call(along_kernel, grid=(groups // per_step,), in_specs=[whole3...  29.9 us
    all_to_all x2, waiting for transfers between devices, send(): lax.all_to_all(x.reshape(groups, -1, width), 'owner', split_axis=0, conca...  22.9 us
    all_to_all x1, blocking collectives, local(): lax.all_to_all(listed, 'owner', split_axis=0, concat_axis=0, tiled=True)  20.7 us
    ppermute x4, waiting for transfers between devices, hop(): return lax.ppermute(x, ('owner', 'dense'), pairs)  19.9 us
    pallas_call x1, Pallas kernels, give_call(): pl.pallas_call(functools.partial(give_kernel, fields, lo, hi), grid=(grou...  13.2 us
    all_to_all x2, starting transfers between devices, send(): lax.all_to_all(x.reshape(groups, -1, width), 'owner', split_axis=0, conca...  12 us
    ppermute x6, waiting for transfers between devices, turn(): lax.ppermute(x, 'dense', [(i, (i + shift) % dense) for i in range(dense)])  10.8 us
    pallas_call x1, Pallas kernels, head_call(): pl.pallas_call(head_kernel, in_specs=[pl.BlockSpec(memory_space=pltpu.SME...  9.69 us
  transfers between devices with their start and end apart: 15, of which 9 were waited for; matrix products, arithmetic and copies ran while one was open for 0% of the time, Pallas kernels for 25%

commit v1 on v0

--- a/solution.py
+++ b/solution.py
@@ -123,14 +123,26 @@
     )(own, loc, w, rank)
 
 
-def take_kernel(flat_ref, tb_ref, out_ref, tt_ref):
-    rows, width = tb_ref.shape
+def turned_kernel(table_ref, list_ref, out_ref):
+    out_ref[...] = table_ref[...].T.astype(bf16)
+
+
+def turned_call(table, listed):
+    rows, width = table.shape
+    vmem = pl.BlockSpec(memory_space=pltpu.VMEM)
+    return pl.pallas_call(
+        turned_kernel,
+        in_specs=[vmem, pl.BlockSpec(memory_space=pl.ANY)],
+        out_specs=vmem,
+        out_shape=jax.ShapeDtypeStruct((width, rows), bf16),
+        compiler_params=params(16),
+        cost_estimate=cost(1 << 31),
+    )(table, listed)
+
+
+def take_kernel(flat_ref, tt_ref, out_ref):
+    rows = tt_ref.shape[1]
     n = flat_ref.shape[1]
-
-    @pl.when(pl.program_id(0) == 0)
-    def _():
-        tt_ref[...] = tb_ref[...].T.astype(bf16)
-
     part = 256
     for k in range(0, n, part):
         asked = flat_ref[:, k : k + part]
@@ -138,23 +150,22 @@
         out_ref[k : k + part, :] = dot(tt_ref[...], marks).T.astype(bf16)
 
 
-def take_call(flat, table):
+def take_call(flat, tt):
     n = flat.shape[1]
-    rows, width = table.shape
+    width, rows = tt.shape
     block = TAKE_BLOCK if n % TAKE_BLOCK == 0 else n
     return pl.pallas_call(
         take_kernel,
         grid=(n // block,),
         in_specs=[
             pl.BlockSpec((1, block), lambda i: (0, i)),
-            pl.BlockSpec((rows, width), lambda i: (0, 0)),
+            pl.BlockSpec((width, rows), lambda i: (0, 0)),
         ],
         out_specs=pl.BlockSpec((block, width), lambda i: (i, 0)),
         out_shape=jax.ShapeDtypeStruct((n, width), bf16),
-        scratch_shapes=[pltpu.VMEM((width, rows), bf16)],
         compiler_params=params(STEP_MIB, ("arbitrary",)),
         cost_estimate=cost(2 * n * rows * width * 2),
-    )(flat, table)
+    )(flat, tt)
 
 
 def build(u_ref, c_ref, cols, first, count, lo, hi):
@@ -469,8 +480,9 @@
     near = hop(w_in)
     listed, rank = list_call(loc, groups)
     lists = lax.all_to_all(listed, "owner", split_axis=0, concat_axis=0, tiled=True)
+    tt = turned_call(table, listed)
     flat = [lists[:, lo:hi].reshape(1, groups * (hi - lo)) for lo, hi in CHUNKS]
-    found = [take_call(a, table) for a in flat]
+    found = [take_call(a, tt) for a in flat]
     rs = [send(x, groups) for x in found]
     u, c = map_call(own, loc, w, after(rank, *found), groups)
 

time: 195 us -> 195 us (level)
  blocking collectives: 20.7 us -> 0 us
  starting transfers between devices: 31.1 us -> 42.7 us
  waiting for transfers between devices: 54.1 us -> 61.1 us
    all_to_all x1 -> x0, blocking collectives: 20.7 us -> none  [local(): lax.all_to_all(listed, 'owner', split_axis=0, concat_axis=0, tiled=True)]
    all_to_all x0 -> x1, starting transfers between devices: none -> 11.6 us  [local(): lax.all_to_all(listed, 'owner', split_axis=0, concat_axis=0, tiled=True)]
    all_to_all x0 -> x1, waiting for transfers between devices: none -> 6.98 us  [local(): lax.all_to_all(listed, 'owner', split_axis=0, concat_axis=0, tiled=True)]
    unnamed x48 -> x52, local copies, waits for them, and re-layouts: 7.06 us -> 8.88 us
  transfers between devices with their start and end apart: 15 -> 16, of which waited for: 9 -> 10; matrix products, arithmetic and copies ran while one was open for 0% -> 0% of each run, Pallas kernels for 25% -> 25%
where the time goes in v1:
time: 195 us; the launch traced here: 194 us
  Pallas kernels  77.8 us (40%)
  waiting for transfers between devices  61.1 us (31%)
  starting transfers between devices  42.7 us (22%)
  local copies, waits for them, and re-layouts  9.39 us (5%)
  other arithmetic  2.46 us (1%)
    pallas_call x1, Pallas kernels, along_call(): pl.pallas_call(along_kernel, grid=(groups // per_step,), in_specs=[whole3...  29.9 us
    all_to_all x2, waiting for transfers between devices, send(): lax.all_to_all(x.reshape(groups, -1, width), 'owner', split_axis=0, conca...  22.9 us
    ppermute x4, waiting for transfers between devices, hop(): return lax.ppermute(x, ('owner', 'dense'), pairs)  19.9 us
    pallas_call x1, Pallas kernels, give_call(): pl.pallas_call(functools.partial(give_kernel, fields, lo, hi), grid=(grou...  13.2 us
    all_to_all x2, starting transfers between devices, send(): lax.all_to_all(x.reshape(groups, -1, width), 'owner', split_axis=0, conca...  12 us
    all_to_all x1, starting transfers between devices, local(): lax.all_to_all(listed, 'owner', split_axis=0, concat_axis=0, tiled=True)  11.6 us
    ppermute x6, waiting for transfers between devices, turn(): lax.ppermute(x, 'dense', [(i, (i + shift) % dense) for i in range(dense)])  10.8 us
    pallas_call x1, Pallas kernels, head_call(): pl.pallas_call(head_kernel, in_specs=[pl.BlockSpec(memory_space=pltpu.SME...  9.69 us
  transfers between devices with their start and end apart: 16, of which 10 were waited for; matrix products, arithmetic and copies ran while one was open for 0% of the time, Pallas kernels for 25%

profile of v1, /device:TPU:1, one launch (start us, length us, event | category | flops | bytes accessed | tf_op | source)
XLA Modules:
  0.0 194.4 jit_solution(14879298371098146399)
XLA Ops:
  0.6 3.6 %collective-permute-start = (bf16[1664,1024]{1,0:T(8,128)(2,1)}, bf16[1664,1024]{1,0:T(8,128)(2,1)S(1)}, u32[]{:S(2)}, u32[]{:S(2)}) collective-permute-start(bf16[1664,1024]{1,0:T(8,128)(2,1)} %own_ref.1), channel_id=1, source_target_pairs={{0,1},{1,2},{2,3},{3,0},{4,7},{5,4},{6,5},{7,6},{8,9},{9,10},{10,1... | collective-permute-start | bytes 10223624 | tf_op jit(solution)/shard_map/ppermute | solution.py:466
  5.1 2.5 %shard_map.112 = (s32[64,128]{1,0:T(8,128)}, f32[16,128]{1,0:T(8,128)S(1)}) custom-call(s32[13,4,256]{2,1,0:T(4,128)S(1)} %bitcast.23), custom_call_target="tpu_custom_call" | custom-call | flops 1048576 | bytes 1024 | tf_op jit(solution)/shard_map/pallas_call | solution.py:76
  7.6 11.6 %all-to-all-start = ((s32[64,1,128]{2,1,0:T(1,128)}), s32[64,1,128]{2,1,0:T(1,128)S(1)}, u32[]{:S(2)}, u32[]{:S(2)}) async-start(s32[64,1,128]{2,1,0:T(1,128)} %bitcast.2), calls=%async_computation | async-start | bytes 65536 | tf_op jit(solution)/shard_map/all_to_all | solution.py:482
  19.2 1.2 copy-done.1
  21.4 7.0 %all-to-all-done = s32[64,1,128]{2,1,0:T(1,128)S(1)} async-done(((s32[64,1,128]{2,1,0:T(1,128)}), s32[64,1,128]{2,1,0:T(1,128)S(1)}, u32[]{:S(2)}, u32[]{:S(2)}) %all-to-all-start) | async-done | bytes 32800 | tf_op jit(solution)/shard_map/all_to_all | solution.py:482
  28.5 1.0 copy-done.8
  29.5 4.5 %shard_map.114 = bf16[6656,128]{1,0:T(8,128)(2,1)S(1)} custom-call(s32[1,6656]{1,0:T(1,128)S(1)} %reshape.24.flat_ref, bf16[128,2048]{1,0:T(8,128)(2,1)S(1)} %copy-done.8), custom_call_target="tpu_custom_call" | custom-call | flops 1048576 | bytes 1024 | tf_op jit(solution)/shard_map/pallas_call | solution.py:157
  34.1 1.2 copy-done
  35.3 5.7 %all-to-all-start.1 = ((bf16[64,104,128]{2,1,0:T(8,128)(2,1)}), bf16[64,104,128]{2,1,0:T(8,128)(2,1)}, u32[]{:S(2)}, u32[]{:S(2)}) async-start(bf16[64,104,128]{2,1,0:T(8,128)(2,1)} %bitcast.15), calls=%async_computation.1 | async-start | bytes 3407872 | tf_op jit(solution)/shard_map/all_to_all | solution.py:453
  41.8 2.3 %shard_map.115 = (f32[64,3328]{1,0:T(8,128)S(1)}, f32[64,3328]{1,0:T(8,128)S(1)}) custom-call(s32[13,4,256]{2,1,0:T(4,128)S(1)} %bitcast.19, s32[13,4,256]{2,1,0:T(4,128)S(1)} %bitcast.24, f32[13,4,256]{2,1,0:T(4,128)S(1)} %bitcast.21, f32[16,128]{1,0:T(8,128)S(1)} %get-tuple-element.17.rank_ref), custom_call_target="tpu_custom_call" | custom-call | flops 1048576 | bytes 1024 | tf_op jit(solution)/shard_map/pallas_call | solution.py:115
  45.0 0.9 copy-done.12
  48.0 2.0 %collective-permute-start.2 = (bf16[16,1024]{1,0:T(8,128)(2,1)S(1)}, bf16[16,1024]{1,0:T(8,128)(2,1)S(1)}, u32[]{:S(2)}, u32[]{:S(2)}) collective-permute-start(bf16[16,1024]{1,0:T(8,128)(2,1)S(1)} %maximum_maximum_fusion), channel_id=1, source_target_pairs={{0,1},{1,2},{2,3},{3,0},{4,7},{5,4},{6,5},{7,6},{8,9},{9,10},{10,1... | collective-permute-start | bytes 98312 | tf_op jit(solution)/shard_map/ppermute | solution.py:466
  50.0 17.6 %collective-permute-done.2 = bf16[16,1024]{1,0:T(8,128)(2,1)S(1)} collective-permute-done((bf16[16,1024]{1,0:T(8,128)(2,1)S(1)}, bf16[16,1024]{1,0:T(8,128)(2,1)S(1)}, u32[]{:S(2)}, u32[]{:S(2)}) %collective-permute-start.2) | collective-permute-done | bytes 32800 | tf_op jit(solution)/shard_map/ppermute | solution.py:466
  67.6 2.6 %collective-permute-start.3 = (bf16[16,1024]{1,0:T(8,128)(2,1)S(1)}, bf16[16,1024]{1,0:T(8,128)(2,1)S(1)}, u32[]{:S(2)}, u32[]{:S(2)}) collective-permute-start(bf16[16,1024]{1,0:T(8,128)(2,1)S(1)} %collective-permute-done.2), channel_id=1, source_target_pairs={{0,4},{4,0},{8,12},{12,8},{16,20},{20,16},{24,28},{28,24},{32,36},... | collective-permute-start | bytes 98312 | tf_op jit(solution)/shard_map/ppermute | solution.py:470
  71.0 2.3 %collective-permute-done.4 = bf16[16,1024]{1,0:T(8,128)(2,1)S(1)} collective-permute-done((bf16[16,1024]{1,0:T(8,128)(2,1)S(1)}, bf16[16,1024]{1,0:T(8,128)(2,1)S(1)}, u32[]{:S(2)}, u32[]{:S(2)}) %collective-permute-start.4) | collective-permute-done | bytes 32800 | tf_op jit(solution)/shard_map/ppermute | solution.py:466
  73.4 10.2 %all-to-all-done.1 = bf16[64,104,128]{2,1,0:T(8,128)(2,1)} async-done(((bf16[64,104,128]{2,1,0:T(8,128)(2,1)}), bf16[64,104,128]{2,1,0:T(8,128)(2,1)}, u32[]{:S(2)}, u32[]{:S(2)}) %all-to-all-start.1) | async-done | bytes 1703968 | tf_op jit(solution)/shard_map/all_to_all | solution.py:453
  83.6 9.2 %shard_map.116.x_ref = bf16[256,1664]{1,0:T(8,128)(2,1)} custom-call(f32[64,3328]{1,0:T(8,128)} %copy-done.4, f32[64,3328]{1,0:T(8,128)} %copy-done.12, bf16[6656,128]{1,0:T(8,128)(2,1)} %bitcast.8.r_ref.refs_0_), custom_call_target="tpu_custom_call" | custom-call | flops 17179869184 | bytes 1024 | tf_op jit(solution)/shard_map/pallas_call | solution.py:218
  92.8 1.1 copy-done.9
  93.9 9.7 %shard_map.117 = (bf16[1664,256]{1,0:T(8,128)(2,1)S(1)}, bf16[3328,128]{1,0:T(8,128)(2,1)S(1)}) custom-call(s32[1]{0:T(128)} %bitcast.6.core_ref, bf16[256,1664]{1,0:T(8,128)(2,1)S(1)} %copy-done.9, f32[1,256]{1,0:T(1,128)S(1)} %bitcast.25, bf16[64,1024]{1,0:T(8,128)(2,1)S(1)} %pad_maximum_fusion.bw_ref, bf16[1664,1024]{1,0:T(8,128)(2,1)S(1)} %copy-done.3, ...), custom_call_target="tpu_custom_call" | custom-call | flops 1048576 | bytes 1024 | tf_op jit(solution)/shard_map/pallas_call | solution.py:287
  103.6 13.2 %shard_map.118 = bf16[6656,128]{1,0:T(8,128)(2,1)} custom-call(f32[64,3328]{1,0:T(8,128)S(1)} %copy-done.5, f32[64,3328]{1,0:T(8,128)S(1)} %copy-done.13, bf16[3328,128]{1,0:T(8,128)(2,1)S(1)} %get-tuple-element.23.d_ref), custom_call_target="tpu_custom_call" | custom-call | flops 1048576 | bytes 1024 | tf_op jit(solution)/shard_map/pallas_call | solution.py:323
  116.9 6.3 %all-to-all-start.2 = ((bf16[64,104,128]{2,1,0:T(8,128)(2,1)}), bf16[64,104,128]{2,1,0:T(8,128)(2,1)S(1)}, u32[]{:S(2)}, u32[]{:S(2)}) async-start(bf16[64,104,128]{2,1,0:T(8,128)(2,1)} %bitcast.10), calls=%async_computation.2 | async-start | bytes 3407872 | tf_op jit(solution)/shard_map/all_to_all | solution.py:453
  123.3 29.9 %shard_map.119 = f32[13,4,256]{2,1,0:T(4,128)} custom-call(s32[13,4,256]{2,1,0:T(4,128)S(1)} %bitcast.20, f32[13,4,256]{2,1,0:T(4,128)S(1)} %bitcast.22, f32[64,3328]{1,0:T(8,128)S(1)} %copy-done.6, bf16[1664,256]{1,0:T(8,128)(2,1)S(1)} %copy-done.11, bf16[6656,128]{1,0:T(8,128)(2,1)} %bitcast.8.r_ref.refs_0_), custom_call_target="tpu_custom_call" | custom-call | flops 1048576 | bytes 1024 | tf_op jit(solution)/shard_map/pallas_call | solution.py:386
  153.1 12.7 %all-to-all-done.2 = bf16[64,104,128]{2,1,0:T(8,128)(2,1)S(1)} async-done(((bf16[64,104,128]{2,1,0:T(8,128)(2,1)}), bf16[64,104,128]{2,1,0:T(8,128)(2,1)S(1)}, u32[]{:S(2)}, u32[]{:S(2)}) %all-to-all-start.2) | async-done | bytes 1703968 | tf_op jit(solution)/shard_map/all_to_all | solution.py:453
  165.8 6.4 %shard_map.120 = bf16[2048,128]{1,0:T(8,128)(2,1)S(1)} custom-call(s32[64,128]{1,0:T(8,128)S(1)} %bitcast.18, bf16[6656,128]{1,0:T(8,128)(2,1)S(1)} %bitcast.16), custom_call_target="tpu_custom_call" | custom-call | flops 1048576 | bytes 1024 | tf_op jit(solution)/shard_map/pallas_call | solution.py:435
  173.0 1.4 collective-permute-start.8
  174.4 2.0 %collective-permute-start.9 = (bf16[512,128]{1,0:T(8,128)(2,1)S(1)}, bf16[512,128]{1,0:T(8,128)(2,1)S(1)}, u32[]{:S(2)}, u32[]{:S(2)}) collective-permute-start(bf16[512,128]{1,0:T(8,128)(2,1)S(1)} %get-tuple-element.32), channel_id=1, source_target_pairs={{0,3},{1,0},{2,1},{3,2},{4,7},{5,4},{6,5},{7,6},{8,11},{9,8},{10,9... | collective-permute-start | bytes 393224 | tf_op jit(solution)/shard_map/ppermute | solution.py:460
  176.4 5.0 %collective-permute-done.7 = bf16[512,128]{1,0:T(8,128)(2,1)S(1)} collective-permute-done((bf16[512,128]{1,0:T(8,128)(2,1)S(1)}, bf16[512,128]{1,0:T(8,128)(2,1)S(1)}, u32[]{:S(2)}, u32[]{:S(2)}) %collective-permute-start.7) | collective-permute-done | bytes 131104 | tf_op jit(solution)/shard_map/ppermute | solution.py:460
  181.8 2.2 %collective-permute-start.10 = (bf16[512,128]{1,0:T(8,128)(2,1)S(1)}, bf16[512,128]{1,0:T(8,128)(2,1)S(1)}, u32[]{:S(2)}, u32[]{:S(2)}) collective-permute-start(bf16[512,128]{1,0:T(8,128)(2,1)S(1)} %get-tuple-element.30), channel_id=1, source_target_pairs={{0,1},{1,2},{2,3},{3,0},{4,5},{5,6},{6,7},{7,4},{8,9},{9,10},{10,1... | collective-permute-start | bytes 393224 | tf_op jit(solution)/shard_map/ppermute | solution.py:460
  184.0 2.2 %collective-permute-start.11 = (bf16[512,128]{1,0:T(8,128)(2,1)S(1)}, bf16[512,128]{1,0:T(8,128)(2,1)S(1)}, u32[]{:S(2)}, u32[]{:S(2)}) collective-permute-start(bf16[512,128]{1,0:T(8,128)(2,1)S(1)} %get-tuple-element.30), channel_id=1, source_target_pairs={{0,2},{1,3},{2,0},{3,1},{4,6},{5,7},{6,4},{7,5},{8,10},{9,11},{10,... | collective-permute-start | bytes 393224 | tf_op jit(solution)/shard_map/ppermute | solution.py:460
  186.5 1.3 collective-permute-done.10
  187.8 4.3 %collective-permute-done.11 = bf16[512,128]{1,0:T(8,128)(2,1)S(1)} collective-permute-done((bf16[512,128]{1,0:T(8,128)(2,1)S(1)}, bf16[512,128]{1,0:T(8,128)(2,1)S(1)}, u32[]{:S(2)}, u32[]{:S(2)}) %collective-permute-start.11) | collective-permute-done | bytes 131104 | tf_op jit(solution)/shard_map/ppermute | solution.py:460
  193.1 1.3 fusion.1
  (79 shorter events, 9.2 us)
Async XLA Ops:
  0.6 45.3 %collective-permute-start = (bf16[1664,1024]{1,0:T(8,128)(2,1)}, bf16[1664,1024]{1,0:T(8,128)(2,1)S(1)}, u32[]{:S(2)}, u32[]{:S(2)}) collective-permute-start(bf16[1664,1024]{1,0:T(8,128)(2,1)} %own_ref.1), channel_id=1, source_target_pairs={{0,1},{1,2},{2,3},{3,0},{4,7},{5,4},{6,5},{7,6},{8,9},{9,10},{10,1... | collective-permute-start | bytes 10223624 | tf_op jit(solution)/shard_map/ppermute | solution.py:466
  7.6 20.8 %all-to-all-start = ((s32[64,1,128]{2,1,0:T(1,128)}), s32[64,1,128]{2,1,0:T(1,128)S(1)}, u32[]{:S(2)}, u32[]{:S(2)}) async-start(s32[64,1,128]{2,1,0:T(1,128)} %bitcast.2), calls=%async_computation | async-start | bytes 65536 | tf_op jit(solution)/shard_map/all_to_all | solution.py:482
  28.4 6.9 %copy-start.14 = (s32[64,1,128]{2,1,0:T(1,128)}, s32[64,1,128]{2,1,0:T(1,128)S(1)}, u32[]{:S(2)}) copy-start(s32[64,1,128]{2,1,0:T(1,128)S(1)} %all-to-all-done) | copy-start | bytes 98308
  35.3 5.7 %copy-start.16 = (s32[256,13,4]{0,2,1:T(4,128)S(1)}, s32[256,13,4]{0,2,1:T(4,128)}, u32[]{:S(2)}) copy-start(s32[256,13,4]{0,2,1:T(4,128)} %param.9) | copy-start | bytes 159748
  35.3 5.7 %copy-start.18 = (f32[256,13,4]{0,2,1:T(4,128)S(1)}, f32[256,13,4]{0,2,1:T(4,128)}, u32[]{:S(2)}) copy-start(f32[256,13,4]{0,2,1:T(4,128)} %param.11) | copy-start | bytes 159748
  35.3 48.3 %all-to-all-start.1 = ((bf16[64,104,128]{2,1,0:T(8,128)(2,1)}), bf16[64,104,128]{2,1,0:T(8,128)(2,1)}, u32[]{:S(2)}, u32[]{:S(2)}) async-start(bf16[64,104,128]{2,1,0:T(8,128)(2,1)} %bitcast.15), calls=%async_computation.1 | async-start | bytes 3407872 | tf_op jit(solution)/shard_map/all_to_all | solution.py:453
  45.9 1.9 copy-start.24
  45.9 24.3 %copy-start.25 = (bf16[256]{0:T(256)(128)(2,1)S(1)}, bf16[256]{0:T(256)(128)(2,1)}, u32[]{:S(2)}) copy-start(bf16[256]{0:T(256)(128)(2,1)} %param.12) | copy-start | bytes 1540
  46.1 24.1 %collective-permute-start.1 = (bf16[832,1024]{1,0:T(8,128)(2,1)S(1)}, bf16[832,1024]{1,0:T(8,128)(2,1)}, u32[]{:S(2)}, u32[]{:S(2)}) collective-permute-start(bf16[832,1024]{1,0:T(8,128)(2,1)S(1)} %constant_dynamic-slice_fusion.3), channel_id=1, source_target_pairs={{0,1},{1,2},{2,3},{3,0},{4,7},{5,4},{6,5},{7,6},{8,9},{9,10},{10,1... | collective-permute-start | bytes 5111816 | tf_op jit(solution)/shard_map/ppermute | solution.py:466
  46.9 45.8 %collective-permute-start.5 = (bf16[1664,1024]{1,0:T(8,128)(2,1)S(1)}, bf16[1664,1024]{1,0:T(8,128)(2,1)}, u32[]{:S(2)}, u32[]{:S(2)}) collective-permute-start(bf16[1664,1024]{1,0:T(8,128)(2,1)S(1)} %collective-permute-done.near_ref), channel_id=1, source_target_pairs={{0,4},{4,0},{8,12},{12,8},{16,20},{20,16},{24,28},{28,24},{32,36},... | collective-permute-start | bytes 10223624 | tf_op jit(solution)/shard_map/ppermute | solution.py:470
  48.0 19.6 %collective-permute-start.2 = (bf16[16,1024]{1,0:T(8,128)(2,1)S(1)}, bf16[16,1024]{1,0:T(8,128)(2,1)S(1)}, u32[]{:S(2)}, u32[]{:S(2)}) collective-permute-start(bf16[16,1024]{1,0:T(8,128)(2,1)S(1)} %maximum_maximum_fusion), channel_id=1, source_target_pairs={{0,1},{1,2},{2,3},{3,0},{4,7},{5,4},{6,5},{7,6},{8,9},{9,10},{10,1... | collective-permute-start | bytes 98312 | tf_op jit(solution)/shard_map/ppermute | solution.py:466
  67.6 3.5 %collective-permute-start.3 = (bf16[16,1024]{1,0:T(8,128)(2,1)S(1)}, bf16[16,1024]{1,0:T(8,128)(2,1)S(1)}, u32[]{:S(2)}, u32[]{:S(2)}) collective-permute-start(bf16[16,1024]{1,0:T(8,128)(2,1)S(1)} %collective-permute-done.2), channel_id=1, source_target_pairs={{0,4},{4,0},{8,12},{12,8},{16,20},{20,16},{24,28},{28,24},{32,36},... | collective-permute-start | bytes 98312 | tf_op jit(solution)/shard_map/ppermute | solution.py:470
  70.2 3.2 %collective-permute-start.4 = (bf16[16,1024]{1,0:T(8,128)(2,1)S(1)}, bf16[16,1024]{1,0:T(8,128)(2,1)S(1)}, u32[]{:S(2)}, u32[]{:S(2)}) collective-permute-start(bf16[16,1024]{1,0:T(8,128)(2,1)S(1)} %collective-permute-done.2), channel_id=1, source_target_pairs={{0,1},{1,2},{2,3},{3,0},{4,7},{5,4},{6,5},{7,6},{8,9},{9,10},{10,1... | collective-permute-start | bytes 98312 | tf_op jit(solution)/shard_map/ppermute | solution.py:466
  70.2 22.5 %collective-permute-start.6 = (bf16[832,1024]{1,0:T(8,128)(2,1)}, bf16[832,1024]{1,0:T(8,128)(2,1)}, u32[]{:S(2)}, u32[]{:S(2)}) collective-permute-start(bf16[832,1024]{1,0:T(8,128)(2,1)} %collective-permute-done.1.far_ref), channel_id=1, source_target_pairs={{0,4},{4,0},{8,12},{12,8},{16,20},{20,16},{24,28},{28,24},{32,36},... | collective-permute-start | bytes 5111816 | tf_op jit(solution)/shard_map/ppermute | solution.py:470
  83.6 9.2 %copy-start.3 = (bf16[1664,1024]{1,0:T(8,128)(2,1)S(1)}, bf16[1664,1024]{1,0:T(8,128)(2,1)}, u32[]{:S(2)}) copy-start(bf16[1664,1024]{1,0:T(8,128)(2,1)} %own_ref.1) | copy-start | bytes 10223620
  93.9 9.7 %copy-start.5 = (f32[64,3328]{1,0:T(8,128)S(1)}, f32[64,3328]{1,0:T(8,128)}, u32[]{:S(2)}) copy-start(f32[64,3328]{1,0:T(8,128)} %copy-done.4) | copy-start | bytes 2555908
  93.9 9.7 %copy-start.13 = (f32[64,3328]{1,0:T(8,128)S(1)}, f32[64,3328]{1,0:T(8,128)}, u32[]{:S(2)}) copy-start(f32[64,3328]{1,0:T(8,128)} %copy-done.12) | copy-start | bytes 2555908
  103.6 13.3 %copy-start.10 = (bf16[1664,256]{1,0:T(8,128)(2,1)}, bf16[1664,256]{1,0:T(8,128)(2,1)S(1)}, u32[]{:S(2)}) copy-start(bf16[1664,256]{1,0:T(8,128)(2,1)S(1)} %get-tuple-element.25.dt_ref) | copy-start | bytes 2555908
  116.9 6.4 %copy-start.6 = (f32[64,3328]{1,0:T(8,128)S(1)}, f32[64,3328]{1,0:T(8,128)}, u32[]{:S(2)}) copy-start(f32[64,3328]{1,0:T(8,128)} %copy-done.4) | copy-start | bytes 2555908
  116.9 6.4 %copy-start.11 = (bf16[1664,256]{1,0:T(8,128)(2,1)S(1)}, bf16[1664,256]{1,0:T(8,128)(2,1)}, u32[]{:S(2)}) copy-start(bf16[1664,256]{1,0:T(8,128)(2,1)} %copy-done.10) | copy-start | bytes 2555908
  116.9 6.4 %copy-start.17 = (s32[256,13,4]{0,2,1:T(4,128)S(1)}, s32[256,13,4]{0,2,1:T(4,128)}, u32[]{:S(2)}) copy-start(s32[256,13,4]{0,2,1:T(4,128)} %param.9) | copy-start | bytes 159748
  116.9 6.4 %copy-start.19 = (f32[256,13,4]{0,2,1:T(4,128)S(1)}, f32[256,13,4]{0,2,1:T(4,128)}, u32[]{:S(2)}) copy-start(f32[256,13,4]{0,2,1:T(4,128)} %param.11) | copy-start | bytes 159748
  116.9 48.9 %all-to-all-start.2 = ((bf16[64,104,128]{2,1,0:T(8,128)(2,1)}), bf16[64,104,128]{2,1,0:T(8,128)(2,1)S(1)}, u32[]{:S(2)}, u32[]{:S(2)}) async-start(bf16[64,104,128]{2,1,0:T(8,128)(2,1)} %bitcast.10), calls=%async_computation.2 | async-start | bytes 3407872 | tf_op jit(solution)/shard_map/all_to_all | solution.py:453
  123.3 42.5 %copy-start.15 = (s32[64,1,128]{2,1,0:T(1,128)S(1)}, s32[64,1,128]{2,1,0:T(1,128)}, u32[]{:S(2)}) copy-start(s32[64,1,128]{2,1,0:T(1,128)} %copy-done.14) | copy-start | bytes 98308
  172.2 20.3 %copy-start.22 = (f32[2048]{0:T(1024)S(1)}, f32[2048]{0:T(1024)}, u32[]{:S(2)}) copy-start(f32[2048]{0:T(1024)} %param.14) | copy-start | bytes 24580
  172.2 20.9 %copy-start.2 = (f32[2048,128]{1,0:T(8,128)S(1)}, f32[2048,128]{1,0:T(8,128)}, u32[]{:S(2)}) copy-start(f32[2048,128]{1,0:T(8,128)} %table_ref.1) | copy-start | bytes 3145732
  172.2 9.2 %collective-permute-start.7 = (bf16[512,128]{1,0:T(8,128)(2,1)S(1)}, bf16[512,128]{1,0:T(8,128)(2,1)S(1)}, u32[]{:S(2)}, u32[]{:S(2)}) collective-permute-start(bf16[512,128]{1,0:T(8,128)(2,1)S(1)} %get-tuple-element.31), channel_id=1, source_target_pairs={{0,1},{1,2},{2,3},{3,0},{4,5},{5,6},{6,7},{7,4},{8,9},{9,10},{10,1... | collective-permute-start | bytes 393224 | tf_op jit(solution)/shard_map/ppermute | solution.py:460
  173.0 8.4 %collective-permute-start.8 = (bf16[512,128]{1,0:T(8,128)(2,1)S(1)}, bf16[512,128]{1,0:T(8,128)(2,1)S(1)}, u32[]{:S(2)}, u32[]{:S(2)}) collective-permute-start(bf16[512,128]{1,0:T(8,128)(2,1)S(1)} %get-tuple-element.33), channel_id=1, source_target_pairs={{0,2},{1,3},{2,0},{3,1},{4,6},{5,7},{6,4},{7,5},{8,10},{9,11},{10,... | collective-permute-start | bytes 393224 | tf_op jit(solution)/shard_map/ppermute | solution.py:460
  174.4 7.2 %collective-permute-start.9 = (bf16[512,128]{1,0:T(8,128)(2,1)S(1)}, bf16[512,128]{1,0:T(8,128)(2,1)S(1)}, u32[]{:S(2)}, u32[]{:S(2)}) collective-permute-start(bf16[512,128]{1,0:T(8,128)(2,1)S(1)} %get-tuple-element.32), channel_id=1, source_target_pairs={{0,3},{1,0},{2,1},{3,2},{4,7},{5,4},{6,5},{7,6},{8,11},{9,8},{10,9... | collective-permute-start | bytes 393224 | tf_op jit(solution)/shard_map/ppermute | solution.py:460
  181.8 5.9 %collective-permute-start.10 = (bf16[512,128]{1,0:T(8,128)(2,1)S(1)}, bf16[512,128]{1,0:T(8,128)(2,1)S(1)}, u32[]{:S(2)}, u32[]{:S(2)}) collective-permute-start(bf16[512,128]{1,0:T(8,128)(2,1)S(1)} %get-tuple-element.30), channel_id=1, source_target_pairs={{0,1},{1,2},{2,3},{3,0},{4,5},{5,6},{6,7},{7,4},{8,9},{9,10},{10,1... | collective-permute-start | bytes 393224 | tf_op jit(solution)/shard_map/ppermute | solution.py:460
  184.0 8.1 %collective-permute-start.11 = (bf16[512,128]{1,0:T(8,128)(2,1)S(1)}, bf16[512,128]{1,0:T(8,128)(2,1)S(1)}, u32[]{:S(2)}, u32[]{:S(2)}) collective-permute-start(bf16[512,128]{1,0:T(8,128)(2,1)S(1)} %get-tuple-element.30), channel_id=1, source_target_pairs={{0,2},{1,3},{2,0},{3,1},{4,6},{5,7},{6,4},{7,5},{8,10},{9,11},{10,... | collective-permute-start | bytes 393224 | tf_op jit(solution)/shard_map/ppermute | solution.py:460
  186.2 5.9 %collective-permute-start.12 = (bf16[512,128]{1,0:T(8,128)(2,1)S(1)}, bf16[512,128]{1,0:T(8,128)(2,1)S(1)}, u32[]{:S(2)}, u32[]{:S(2)}) collective-permute-start(bf16[512,128]{1,0:T(8,128)(2,1)S(1)} %get-tuple-element.30), channel_id=1, source_target_pairs={{0,3},{1,0},{2,1},{3,2},{4,7},{5,4},{6,5},{7,6},{8,11},{9,8},{10,9... | collective-permute-start | bytes 393224 | tf_op jit(solution)/shard_map/ppermute | solution.py:460
  (10 other events, 10.7 us)
